TPU v7x, 512 devices: a whole 4x4x16 slice. The times are simulated.
512 devices in a mesh: dp: 32 (over z, y_lo), module: 16 (over x, y_hi, core).
Axes of the slice: x: 4, y: 4 (y_hi: 2, y_lo: 2; y = y_hi * 2 + y_lo), z: 16, core: 2. Of those that a mesh axis runs over, the one named last changes fastest.
Arguments:
- act_factors: bfloat16 [8192, 16, 32, 128], P(('dp', 'module')), may hold values from -6 to 6
- grad_factors: bfloat16 [8192, 16, 32, 128], P(('dp', 'module')), may hold values from -6 to 6
- lengths: int32 [8192], P(('dp', 'module')), may hold values from 1 to 128, 786432 in all
- module_slot: int32 [16], replicated, may hold values from 0 to 15, each once
- query_grads: float32 [16, 1024, 512], P('module', 'dp'), may hold values from -4 to 4
Outputs:
- scores: float32 [8192, 512], P('dp', 'module')
Inputs may be any that keep to these rules, and one draw needn't show every extreme that they name: `module_slot`: each module is held by exactly one index of the module axis. `lengths`: some example has all 128 tokens.
All inputs are finite; a program needn't handle non-finite values. No bound on the sum of `lengths` on one device may be relied on, other than what follows from the above.
Results may differ from a plain program's by a relative error of at most 0.007.
Values may be sent and summed in bfloat16 or wider, within the bound.
A program may use at most 64 MiB of HBM per device.

v0:
```python
import jax
import jax.numpy as jnp
from jax import lax
from jax.sharding import PartitionSpec as P

ITERS = 4


def chebyshev(rhs, multiply, damping, upper):
    center = (upper + damping) / 2.0
    radius = (upper - damping) / 2.0
    sigma = center / radius
    rho = 1.0 / sigma
    resid = rhs
    step = rhs / center
    solved = jnp.zeros_like(rhs)
    for index in range(ITERS):
        solved = solved + step
        if index + 1 < ITERS:
            resid = resid - (multiply(step) + damping * step)
            rho_next = 1.0 / (2.0 * sigma - rho)
            step = rho_next * rho * step + 2.0 * rho_next / radius * resid
            rho = rho_next
    return solved


def per_device(act_factors, grad_factors, lengths, module_slot, query_grads):
    ex_dev, mods, rank, span = act_factors.shape
    proj = rank * rank
    positions = lax.broadcasted_iota(jnp.int32, (ex_dev, span), 1)
    live = (positions < lengths[:, None]).astype(jnp.bfloat16)
    masked = act_factors * live[:, None, None, :]
    outer = jnp.einsum("emil,emjl->emij", masked, grad_factors, preferred_element_type=jnp.float32)
    per_example = outer.reshape(ex_dev, mods, proj).astype(jnp.bfloat16)
    placing = (module_slot[None, :] == lax.broadcasted_iota(jnp.int32, (mods, mods), 0)).astype(
        jnp.bfloat16
    )
    ordered = jnp.einsum(
        "jm,emp->ejp", placing, per_example, preferred_element_type=jnp.float32
    ).astype(jnp.bfloat16)
    owned = lax.all_to_all(ordered, "module", split_axis=1, concat_axis=0, tiled=True)
    train = owned.reshape(owned.shape[0], proj)
    n_data = lax.axis_size("dp")
    n_mod = lax.axis_size("module")
    examples = train.shape[0] * n_data
    band = proj // n_data
    columns = train
    gram_rows = (
        lax.psum_scatter(
            lax.dot_general(
                columns, train, (((0,), (0,)), ((), ())), preferred_element_type=jnp.float32
            ),
            "dp",
            scatter_dimension=0,
            tiled=True,
        )
        / examples
    )
    own_slot = (lax.broadcasted_iota(jnp.int32, (n_mod,), 0) == lax.axis_index("module")).astype(
        jnp.float32
    )
    first = lax.axis_index("dp") * band
    on_diagonal = (
        lax.broadcasted_iota(jnp.int32, (band, proj), 1)
        == lax.broadcasted_iota(jnp.int32, (band, proj), 0) + first
    )
    local_trace = jnp.sum(jnp.where(on_diagonal, gram_rows, 0.0))
    traces = lax.psum(own_slot * local_trace, ("dp", "module"))
    mean_eig = traces / proj
    damping = 0.1 * jnp.mean(mean_eig)
    upper = damping + 4.0 * jnp.sum(mean_eig * own_slot)
    queries = query_grads[0]

    def spread(step):
        return jnp.dot(
            gram_rows,
            lax.all_gather(step, "dp", axis=0, tiled=True),
            precision=lax.Precision.HIGHEST,
            preferred_element_type=jnp.float32,
        )

    solved = chebyshev(queries, spread, damping, upper).astype(jnp.bfloat16)
    columns = train
    partial_scores = jnp.dot(
        columns,
        lax.all_gather(solved, "dp", axis=0, tiled=True),
        preferred_element_type=jnp.float32,
    )
    gathered = lax.all_to_all(
        partial_scores[None].astype(jnp.bfloat16), "module", split_axis=2, concat_axis=0, tiled=True
    ).astype(jnp.float32)
    return jnp.sum(gathered, axis=0)


def solution(mesh):
    return jax.shard_map(
        per_device,
        mesh=mesh,
        in_specs=(
            P(("dp", "module"), None, None, None),
            P(("dp", "module"), None, None, None),
            P(("dp", "module")),
            P(),
            P("module", "dp", None),
        ),
        out_specs=P("dp", "module"),
        check_vma=False,
    )
```

profile of v0, /device:TPU:1, one launch (start us, length us, event | category | flops | bytes accessed | tf_op | source)
XLA Modules:
  0.0 853.5 jit_solution(11290084339213597308)
XLA Ops:
  6.5 0.0 copy-start
  6.5 0.0 reduce-scatter.2.cloned.1.call-start
  6.5 0.9 fusion.23
  7.4 0.7 copy-done
  8.1 4.1 fusion.2
  12.3 0.0 copy-start.4
  12.3 3.5 convert_element_type.40
  15.8 0.0 copy-done.4
  15.8 0.3 fusion.5
  16.1 0.3 copy.12
  16.4 20.5 %all_to_all.24 = bf16[16,16,1024]{2,0,1:T(8,128)(2,1)S(1)} all-to-all(bf16[16,16,1024]{2,0,1:T(8,128)(2,1)S(1)} %copy.12), channel_id=1, replica_groups=mesh['dp'=32,'module'=16] {'module'}, dimensions={1} | all-to-all | bytes 1048576 | tf_op jit(solution)/shard_map/all_to_all | solution.py:41
  36.9 3.1 convolution_bitcast_fusion
  40.1 0.0 copy-start.3
  40.1 0.0 reduce-scatter.2.cloned.1.call-update
  40.1 0.0 all-gather.5.cloned.1.call-start
  40.2 122.1 %reduce-scatter.2.cloned.1.call-done = f32[32,1024]{1,0:T(8,128)} async-done(((f32[1024,1024]{1,0:T(8,128)}), f32[32,1024]{1,0:T(8,128)}) %reduce-scatter.2.cloned.1.call-update) | async-done | bytes 131088 | tf_op jit(solution)/shard_map/reduce_scatter | solution.py:49
  162.3 0.0 copy-start.1
  162.3 1.7 select_reduce_fusion
  163.9 0.6 compare_select_fusion.1
  164.6 123.6 %psum.7 = f32[16]{0:T(128)S(1)} all-reduce(f32[16]{0:T(128)S(1)} %compare_select_fusion.1), channel_id=1, replica_groups=mesh['dp'=32,'module'=16] {'dp','module'}, use_global_device_ids=true, to_apply=%region_2.3 | all-reduce | flops 16 | bytes 128 | tf_op jit(solution)/shard_map/psum | solution.py:68
  288.2 0.7 fusion.27
  290.2 0.0 copy-done.3
  290.2 0.6 bitcast_divide_fusion
  290.8 0.0 all-gather.5.cloned.1.call-update
  290.8 0.0 all-gather.7.cloned.1.call-start
  291.1 107.4 %all-gather.5.cloned.1.call-done = f32[1024,512]{1,0:T(8,128)} async-done(((f32[32,512]{1,0:T(8,128)}), f32[1024,512]{1,0:T(8,128)}) %all-gather.5.cloned.1.call-update) | async-done | bytes 2097168 | tf_op jit(solution)/shard_map/all_gather | solution.py:77
  398.5 3.6 multiply_add_fusion.1
  402.1 0.0 copy-start.2
  402.1 0.0 all-gather.7.cloned.1.call-update
  402.1 0.0 all-gather.9.cloned.1.call-start
  402.3 132.5 %all-gather.7.cloned.1.call-done = f32[1024,512]{1,0:T(8,128)} async-done(((f32[32,512]{1,0:T(8,128)}), f32[1024,512]{1,0:T(8,128)}) %all-gather.7.cloned.1.call-update) | async-done | bytes 2097168 | tf_op jit(solution)/shard_map/all_gather | solution.py:77
  534.8 0.0 copy-done.1
  534.8 3.5 multiply_add_fusion
  538.3 0.0 all-gather.9.cloned.1.call-update
  538.3 0.0 all-gather.11.cloned.1.call-start
  538.4 132.5 %all-gather.9.cloned.1.call-done = f32[1024,512]{1,0:T(8,128)} async-done(((f32[32,512]{1,0:T(8,128)}), f32[1024,512]{1,0:T(8,128)}) %all-gather.9.cloned.1.call-update) | async-done | bytes 2097168 | tf_op jit(solution)/shard_map/all_gather | solution.py:77
  670.9 0.0 copy-done.2
  670.9 3.5 fusion.13
  674.4 0.0 all-gather.11.cloned.1.call-update
  674.5 0.3 copy.22
  674.8 0.3 copy.14
  675.1 129.1 %all-gather.11.cloned.1.call-done = bf16[1024,512]{1,0:T(8,128)(2,1)} async-done(((bf16[32,512]{1,0:T(8,128)(2,1)}), bf16[1024,512]{1,0:T(8,128)(2,1)}) %all-gather.11.cloned.1.call-update) | async-done | bytes 1048592 | tf_op jit(solution)/shard_map/all_gather | solution.py:86
  804.2 1.7 fusion.6
  805.8 0.4 copy.15
  806.3 0.5 broadcast.25
  806.8 2.2 reduce.3
  809.0 0.1 reshape.37
  809.1 36.9 %all_to_all.25 = bf16[16,2,4096]{2,1,0:T(2,128)(2,1)S(1)} all-to-all(bf16[16,2,4096]{2,1,0:T(2,128)(2,1)S(1)} %reshape.37), channel_id=1, replica_groups=mesh['dp'=32,'module'=16] {'module'}, dimensions={0} | all-to-all | bytes 524288 | tf_op jit(solution)/shard_map/all_to_all | solution.py:89
  846.0 0.3 reshape.38
  846.3 0.7 convert_reduce_fusion
  (2 shorter events, 0.0 us)
Async XLA Ops:
  6.5 1.6 copy-start
  6.5 155.7 %reduce-scatter.2.cloned.1.call-start = ((), (), s32[]{:S(2)}) async-start(), calls=%async_computation.3 | async-start | bytes 4325376 | tf_op jit(solution)/shard_map/reduce_scatter | solution.py:49
  12.3 3.5 copy-start.4
  40.1 250.1 %copy-start.3 = (f32[1,32,512]{2,1,0:T(8,128)S(1)}, f32[1,32,512]{2,1,0:T(8,128)}, u32[]{:S(2)}) copy-start(f32[1,32,512]{2,1,0:T(8,128)} %param.9) | copy-start | bytes 196612
  40.1 358.4 %all-gather.5.cloned.1.call-start = ((), (), s32[]{:S(2)}) async-start(), calls=%async_computation.4 | async-start | bytes 2162688 | tf_op jit(solution)/shard_map/all_gather | solution.py:77
  162.3 372.5 %copy-start.1 = (f32[32,1024]{1,0:T(8,128)S(1)}, f32[32,1024]{1,0:T(8,128)}, u32[]{:S(2)}) copy-start(f32[32,1024]{1,0:T(8,128)} %reduce-scatter.2.cloned.1.call-done) | copy-start | bytes 393220
  290.8 243.9 %all-gather.7.cloned.1.call-start = ((), (), s32[]{:S(2)}) async-start(), calls=%async_computation.5 | async-start | bytes 2162688 | tf_op jit(solution)/shard_map/all_gather | solution.py:77
  402.1 268.8 %copy-start.2 = (f32[32,512]{1,0:T(8,128)S(1)}, f32[32,512]{1,0:T(8,128)}, u32[]{:S(2)}) copy-start(f32[32,512]{1,0:T(8,128)} %get-tuple-element.7) | copy-start | bytes 196612
  402.1 268.8 %all-gather.9.cloned.1.call-start = ((), (), s32[]{:S(2)}) async-start(), calls=%async_computation.6 | async-start | bytes 2162688 | tf_op jit(solution)/shard_map/all_gather | solution.py:77
  538.3 265.9 %all-gather.11.cloned.1.call-start = ((), (), s32[]{:S(2)}) async-start(), calls=%async_computation.7 | async-start | bytes 1081344 | tf_op jit(solution)/shard_map/all_gather | solution.py:86
Sparse Core Ops, SparseCore 0:
  40.2 122.0 reduce-scatter.1
  291.0 107.4 all-gather.4
  402.3 132.4 all-gather.6
  538.4 132.4 all-gather.8
  674.6 129.5 all-gather.10
where the time goes:
time: 854 us; the launch traced here: 853 us
  waiting for transfers between devices  624 us (73%)
  blocking collectives  181 us (21%)
  matrix products  19.9 us (2%)
  between operations  14.9 us (2%)
    all_gather x3, waiting for transfers between devices, spread(): lax.all_gather(step, 'dp', axis=0, tiled=True)  372 us
    all_gather x1, waiting for transfers between devices, per_device(): lax.all_gather(solved, 'dp', axis=0, tiled=True)  129 us
    psum x1, blocking collectives, per_device(): traces = lax.psum(own_slot * local_trace, ('dp', 'module'))  124 us
    reduce_scatter x1, waiting for transfers between devices, per_device(): lax.psum_scatter(lax.dot_general(columns, train, (((0,), (0,)), ((), ()))...  122 us
    all_to_all x1, blocking collectives, per_device(): lax.all_to_all(partial_scores[None].astype(jnp.bfloat16), 'module', split...  36.9 us
    all_to_all x1, blocking collectives, per_device(): lax.all_to_all(ordered, 'module', split_axis=1, concat_axis=0, tiled=True)  20.5 us
  transfers between devices with their start and end apart: 5, of which 5 were waited for; matrix products, arithmetic and copies ran while one was open for 0% of the time, Pallas kernels for 0%

commit v1 on v0

v1 whole, which is shorter than its diff:
```python
import functools

import jax
import jax.numpy as jnp
from jax import lax
from jax.experimental import pallas as pl
from jax.experimental.pallas import tpu as pltpu
from jax.sharding import PartitionSpec as P

ITERS = 4
MESH = pl.DeviceIdType.MESH
BF16 = jnp.bfloat16
F32 = jnp.float32


def kernel(
    planes,
    slot_ref,
    len_ref,
    act_hbm,
    grad_hbm,
    query_ref,
    out_ref,
    act,
    grad,
    prod,
    tsend,
    tall,
    gpart,
    gfull,
    up_out,
    up_in,
    down_out,
    down_in,
    qsrc,
    qfull,
    step_ref,
    resid_ref,
    acc_ref,
    ssend,
    srecv,
    slot_traces,
    plane_traces,
    diag_ref,
    load_sem,
    t_send,
    t_recv,
    tsib_send,
    tsib_recv,
    q_pair,
    q_send,
    q_recv,
    rs_send,
    rs_recv,
    g_send,
    g_recv,
    tr_send,
    tr_recv,
    trz_send,
    trz_recv,
    s_send,
    s_recv,
):
    per_dev, slots, rank, span = act.shape
    proj = rank * rank
    band = proj // (2 * planes)
    half_band = proj // 2
    rows = slots * per_dev
    queries = qfull.shape[1]
    per_owner = queries // slots
    up_steps = planes // 2
    down_steps = planes - 1 - up_steps
    examples = rows * 2 * planes

    dp, mod = lax.axis_index("dp"), lax.axis_index("module")
    z, y_lo = dp // 2, dp % 2
    core = mod % 2
    slot = (mod // 2) * 2 + y_lo
    above, below = (z + 1) % planes, (z + planes - 1) % planes

    def device(plane, chip, cc):
        return (plane * 2 + chip % 2, (chip // 2) * 2 + cc)

    def remote(src, dst, send, recv, target):
        return pltpu.make_async_remote_copy(
            src_ref=src, dst_ref=dst, send_sem=send, recv_sem=recv,
            device_id=target, device_id_type=MESH,
        )

    sibling = device(z, slot, 1 - core)
    up_dev, down_dev = device(above, slot, core), device(below, slot, core)

    loads = [
        pltpu.make_async_copy(act_hbm, act, load_sem.at[0]),
        pltpu.make_async_copy(grad_hbm, grad, load_sem.at[1]),
    ]
    for load in loads:
        load.start()

    barrier = pltpu.get_barrier_semaphore()

    def greet(index, carry):
        chip, cc = index // 2, index % 2

        @pl.when(jnp.logical_or(chip != slot, cc != core))
        def _():
            pl.semaphore_signal(
                barrier, inc=1, device_id=device(z, chip, cc), device_id_type=MESH
            )

        return carry

    lax.fori_loop(0, 2 * slots, greet, 0)
    for target in (up_dev, down_dev):
        pl.semaphore_signal(barrier, inc=1, device_id=target, device_id_type=MESH)
    qsrc[...] = query_ref[...].astype(BF16)
    pl.semaphore_wait(barrier, 2 * slots + 1)

    def q_rows(plane, cc):
        return qfull.at[pl.ds(pl.multiple_of((plane * 2 + cc) * band, band), band), :]

    paired = remote(
        qsrc,
        qfull.at[pl.ds(pl.multiple_of(dp * band, band), band), :],
        q_pair.at[0],
        q_pair.at[1],
        device(z, (slot // 2) * 2 + core, y_lo),
    )

    @pl.when(y_lo != core)
    def _():
        paired.start()

    @pl.when(y_lo == core)
    def _():
        qfull[pl.ds(pl.multiple_of(dp * band, band), band), :] = qsrc[...]

    def chain(part, send, recv, share):
        def up(t):
            block = part((z + planes - t) % planes, core)
            return remote(block, block, send.at[t], recv.at[t], up_dev)

        def down(t):
            block = part((z + t) % planes, core)
            return remote(
                block, block, send.at[up_steps + t], recv.at[up_steps + t], down_dev
            )

        def up_arrival(t):
            block = part((z + planes - t - 1) % planes, core)
            return remote(block, block, send.at[t], recv.at[t], up_dev)

        def down_arrival(t):
            block = part((z + t + 1) % planes, core)
            return remote(
                block, block, send.at[up_steps + t], recv.at[up_steps + t], down_dev
            )

        base = up_steps + down_steps

        def across(t):
            block = part((z + t) % planes, core)
            return remote(block, block, send.at[base + t], recv.at[base + t], sibling)

        def across_arrival(t):
            block = part((z + t) % planes, 1 - core)
            return remote(block, block, send.at[base + t], recv.at[base + t], sibling)

        def run(t):
            if t > 0:
                up_arrival(t - 1).wait_recv()
            if t < up_steps:
                up(t).start()
            if t > 0 and t - 1 < down_steps:
                down_arrival(t - 1).wait_recv()
            if t < down_steps:
                down(t).start()
            if share:
                if t == 0:
                    across(0).start()
                else:
                    across(planes - t).start()
                    if t - 1 < down_steps:
                        across(t).start()

        def finish():
            for t in range(up_steps):
                up(t).wait_send()
            for t in range(down_steps):
                down(t).wait_send()
            if share:
                for t in range(planes):
                    across_arrival(t).wait_recv()
                    across(t).wait_send()

        return run, finish

    q_run, q_finish = chain(q_rows, q_send, q_recv, True)

    for load in loads:
        load.wait()

    lanes = lax.broadcasted_iota(jnp.int32, (8, 4 * rank), 1) // rank
    positions = lax.broadcasted_iota(jnp.int32, (4 * rank, span), 1)

    def t_rows(chip, cc):
        first = cc * rows + (chip % 2) * (rows // 2) + (chip // 2) * per_dev
        return tall.at[pl.ds(pl.multiple_of(first, per_dev), per_dev), :]

    def holder(chip):
        found = jnp.int32(0)
        for index in range(slots):
            found = jnp.where(slot_ref[index] == chip, index, found)
        return found

    def group(k, carry):
        first = ((slot // 4 + 1 + k) % (slots // 4)) * 4
        held = [holder(first + r) for r in range(4)]
        for e in range(per_dev):
            left = jnp.concatenate([act[e, h] for h in held], axis=0)
            right = jnp.concatenate([grad[e, h] for h in held], axis=0)
            left = jnp.where(positions < len_ref[e], left, jnp.zeros_like(left))
            prod[pl.ds(e * 4 * rank, 4 * rank), :] = lax.dot_general(
                left, right, (((1,), (1,)), ((), ())), preferred_element_type=F32
            )
        for r in range(4):
            chip = first + r
            for g in range(proj // (4 * rank)):
                halves = []
                for h in range(per_dev // 8):
                    merged = None
                    for b in range(4):
                        row = h * 8 * 4 * rank + r * rank + 4 * g + b
                        piece = prod[pl.ds(row, 8, stride=4 * rank), :]
                        if b != r:
                            piece = pltpu.roll(piece, ((b - r) % 4) * rank, 1)
                        merged = piece if merged is None else jnp.where(lanes == b, piece, merged)
                    halves.append(merged)
                tsend[chip, :, pl.ds(g * 4 * rank, 4 * rank)] = jnp.concatenate(
                    halves, axis=0
                ).astype(BF16)

            @pl.when(chip != slot)
            def _():
                remote(
                    tsend.at[chip], t_rows(slot, core), t_send.at[chip], t_recv.at[slot],
                    device(z, chip, core),
                ).start()

            @pl.when(chip == slot)
            def _():
                first_row = core * rows + (slot % 2) * (rows // 2) + (slot // 2) * per_dev
                tall[pl.ds(pl.multiple_of(first_row, per_dev), per_dev), :] = tsend[chip]

        return carry

    lax.fori_loop(0, slots // 4, group, 0)

    @pl.when(y_lo != core)
    def _():
        paired.wait()

    def collect(k, carry):
        chip = (slot + k) % slots

        @pl.when(k > 0)
        def _():
            remote(
                t_rows(chip, core), t_rows(chip, core), t_send.at[chip], t_recv.at[chip], sibling
            ).wait_recv()

        remote(
            t_rows(chip, core), t_rows(chip, core), tsib_send.at[chip], tsib_recv.at[chip], sibling
        ).start()
        return carry

    for t in range(up_steps + 1):
        q_run(t)
    lax.fori_loop(0, slots, collect, 0)

    def collected(chip, carry):
        other = remote(
            t_rows(chip, 1 - core), t_rows(chip, 1 - core), tsib_send.at[chip], tsib_recv.at[chip],
            sibling,
        )
        other.wait_recv()
        other.wait_send()
        return carry

    lax.fori_loop(0, slots, collected, 0)

    mine = pl.ds(pl.multiple_of(core * half_band, half_band), half_band)
    gpart[...] = lax.dot_general(
        tall[:, mine], tall[...], (((0,), (0,)), ((), ())), preferred_element_type=F32
    )
    lane = min(128, half_band)
    off = lax.broadcasted_iota(jnp.int32, (lane, lane), 0) != lax.broadcasted_iota(
        jnp.int32, (lane, lane), 1
    )
    for n in range(half_band // lane):
        cols = pl.ds(pl.multiple_of(core * half_band + n * lane, lane), lane)
        gpart[pl.ds(n * lane, lane), cols] = jnp.where(off, gpart[pl.ds(n * lane, lane), cols], 0.0)

    def owned(plane):
        return gpart[pl.ds(pl.multiple_of(plane * band, band), band), :]

    def rs_up(t):
        return remote(up_out.at[t], up_in.at[t], rs_send.at[t], rs_recv.at[t], up_dev)

    def rs_down(t):
        return remote(
            down_out.at[t], down_in.at[t], rs_send.at[up_steps + t], rs_recv.at[up_steps + t],
            down_dev,
        )

    def trace_to(chip):
        return remote(
            slot_traces.at[slot], slot_traces.at[slot], tr_send.at[chip], tr_recv.at[slot],
            device(z, chip, core),
        )

    def trace_from(chip):
        return remote(
            slot_traces.at[chip], slot_traces.at[chip], tr_send.at[chip], tr_recv.at[chip], sibling
        )

    for t in range(up_steps):
        value = owned((z + up_steps - t) % planes)
        if t > 0:
            rs_up(t - 1).wait_recv()
            value = value + up_in[t - 1].astype(F32)
        up_out[t] = value.astype(BF16)
        rs_up(t).start()
        if t < down_steps:
            value = owned((z + planes - down_steps + t) % planes)
            if t > 0:
                rs_down(t - 1).wait_recv()
                value = value + down_in[t - 1].astype(F32)
            down_out[t] = value.astype(BF16)
            rs_down(t).start()
        if t == 0:
            squares = tall[...].astype(F32)
            squares = jnp.sum(squares * squares, axis=0, keepdims=True)
            for n in range(proj // 128):
                plane_traces[z, pl.ds(n, 1), :] = squares[:, n * 128 : (n + 1) * 128]
            squares = jnp.sum(squares, axis=1, keepdims=True)
            slot_traces[slot] = jnp.broadcast_to(squares, (8, 128))

            def tell(chip, carry):
                @pl.when(chip != slot)
                def _():
                    trace_to(chip).start()

                return carry

            lax.fori_loop(0, slots, tell, 0)

    def heard(chip, carry):
        @pl.when(chip != slot)
        def _():
            trace_from(chip).wait_recv()
            trace_to(chip).wait_send()

        return carry

    lax.fori_loop(0, slots, heard, 0)
    total = jnp.sum(slot_traces[...], axis=0)
    plane_traces[z, pl.ds(proj // 128, 8), :] = total

    def g_rows(plane, cc):
        return gfull.at[pl.ds(pl.multiple_of((cc * planes + plane) * band, band), band), :]

    value = owned(z)
    rs_up(up_steps - 1).wait_recv()
    value = value + up_in[up_steps - 1].astype(F32)
    if down_steps > 0:
        rs_down(down_steps - 1).wait_recv()
        value = value + down_in[down_steps - 1].astype(F32)
    gfull[pl.ds(pl.multiple_of((core * planes + z) * band, band), band), :] = value.astype(BF16)

    g_run, g_finish = chain(g_rows, g_send, g_recv, True)
    trz_run, trz_finish = chain(lambda plane, cc: plane_traces.at[plane], trz_send, trz_recv, False)
    for t in range(up_steps + 1):
        g_run(t)
        trz_run(t)
    for t in range(up_steps):
        rs_up(t).wait_send()
    for t in range(down_steps):
        rs_down(t).wait_send()

    def sent(chip, carry):
        @pl.when(chip != slot)
        def _():
            remote(
                tsend.at[chip], t_rows(slot, core), t_send.at[chip], t_recv.at[slot],
                device(z, chip, core),
            ).wait_send()

        return carry

    lax.fori_loop(0, slots, sent, 0)
    q_finish()
    trz_finish()
    g_finish()

    traces = jnp.sum(plane_traces[...], axis=0)
    diagonal = traces[: proj // 128] / examples
    own_eig = jnp.sum(jnp.sum(diagonal, axis=1, keepdims=True), axis=0, keepdims=True) / proj
    damping = 0.1 * (traces[proj // 128 : proj // 128 + 1, 0:1] / (examples * proj * slots))
    diag_ref[...] = jnp.concatenate([diagonal[n : n + 1] for n in range(proj // 128)], axis=1)
    upper = damping + 4.0 * own_eig
    center = (upper + damping) / 2.0
    radius = (upper - damping) / 2.0
    sigma = center / radius
    rho = 1.0 / sigma
    train = tall[pl.ds(pl.multiple_of(core * rows, rows), rows), :].astype(F32)
    resid_ref[...] = train
    step_ref[...] = train / center
    acc_ref[...] = step_ref[...]
    tile = min(256, proj)
    for index in range(ITERS - 1):
        rho_next = 1.0 / (2.0 * sigma - rho)
        rounded = step_ref[...].astype(BF16)

        def column(n, carry):
            cols = pl.ds(pl.multiple_of(n * tile, tile), tile)
            product = jnp.dot(rounded, gfull[:, cols], preferred_element_type=F32)
            step = step_ref[:, cols]
            resid = resid_ref[:, cols] - (product * (1.0 / examples) + (diag_ref[:, cols] + damping) * step)
            resid_ref[:, cols] = resid
            step = rho_next * rho * step + (2.0 * rho_next / radius) * resid
            step_ref[:, cols] = step
            acc_ref[:, cols] = acc_ref[:, cols] + step
            return carry

        lax.fori_loop(0, proj // tile, column, 0)
        rho = rho_next

    scores = jnp.dot(acc_ref[...].astype(BF16), qfull[...], preferred_element_type=F32)
    ssend[...] = scores.T.astype(BF16)

    def block(index):
        owner, low = index // 2, index % 2
        return ssend.at[
            pl.ds(pl.multiple_of(owner * per_owner, per_owner), per_owner),
            pl.ds(pl.multiple_of(low * (rows // 2), rows // 2), rows // 2),
        ]

    mark = slot * 2 + core

    def score_to(index):
        return remote(
            block(index), srecv.at[mark], s_send.at[index], s_recv.at[mark],
            (z * 2 + index % 2, index // 2),
        )

    own = mod * 2 + y_lo

    def push(k, carry):
        index = (own + k) % (2 * slots)
        score_to(index).start()
        return carry

    lax.fori_loop(1, 2 * slots, push, 0)
    srecv[mark] = ssend[
        pl.ds(pl.multiple_of(mod * per_owner, per_owner), per_owner),
        pl.ds(pl.multiple_of(y_lo * (rows // 2), rows // 2), rows // 2),
    ]

    def pull(k, carry):
        index = (mark + k) % (2 * slots)
        remote(
            srecv.at[index], srecv.at[index], s_send.at[index], s_recv.at[index], sibling
        ).wait_recv()
        return carry

    lax.fori_loop(1, 2 * slots, pull, 0)
    sums = []
    for cc in range(2):
        summed = srecv[cc].astype(F32)
        for chip in range(1, slots):
            summed = summed + srecv[chip * 2 + cc].astype(F32)
        sums.append(summed)
    width = rows // 2
    runs = width // per_dev
    lane_run = lax.broadcasted_iota(jnp.int32, (per_owner, width), 1) // per_dev
    for h in range(2):
        merged = jnp.zeros((per_owner, width), F32)
        for n in range(runs // 2):
            for cc in range(2):
                shift = (2 * n + cc - (h * (runs // 2) + n)) % runs
                piece = pltpu.roll(sums[cc], shift * per_dev, 1) if shift else sums[cc]
                merged = jnp.where(lane_run == 2 * n + cc, piece, merged)
        out_ref[:, pl.ds(h * width, width)] = merged

    def pushed(k, carry):
        score_to((own + k) % (2 * slots)).wait_send()
        return carry

    lax.fori_loop(1, 2 * slots, pushed, 0)


def per_device(planes, act_factors, grad_factors, lengths, module_slot, query_grads):
    per_dev, slots, rank, span = act_factors.shape
    proj = rank * rank
    rows = slots * per_dev
    band, queries = query_grads.shape[1:]
    per_owner = queries // slots
    up_steps = planes // 2
    down_steps = planes - 1 - up_steps
    sem = pltpu.SemaphoreType.DMA
    wide = planes - 1 + planes
    vmem = pltpu.VMEM
    result = pl.pallas_call(
        functools.partial(kernel, planes),
        out_shape=jax.ShapeDtypeStruct((per_owner, rows), F32),
        in_specs=[
            pl.BlockSpec(memory_space=pltpu.SMEM),
            pl.BlockSpec(memory_space=pltpu.SMEM),
            pl.BlockSpec(memory_space=pltpu.HBM),
            pl.BlockSpec(memory_space=pltpu.HBM),
            pl.BlockSpec(memory_space=pltpu.VMEM),
        ],
        out_specs=pl.BlockSpec(memory_space=pltpu.VMEM),
        scratch_shapes=[
            vmem((per_dev, slots, rank, span), BF16),
            vmem((per_dev, slots, rank, span), BF16),
            vmem((per_dev * 4 * rank, 4 * rank), F32),
            vmem((slots, per_dev, proj), BF16),
            vmem((2 * rows, proj), BF16),
            vmem((proj // 2, proj), F32),
            vmem((proj, proj), BF16),
            vmem((up_steps, band, proj), BF16),
            vmem((up_steps, band, proj), BF16),
            vmem((max(down_steps, 1), band, proj), BF16),
            vmem((max(down_steps, 1), band, proj), BF16),
            vmem((band, queries), BF16),
            vmem((proj, queries), BF16),
            vmem((rows, proj), F32),
            vmem((rows, proj), F32),
            vmem((rows, proj), F32),
            vmem((queries, rows), BF16),
            vmem((2 * slots, per_owner, rows // 2), BF16),
            vmem((slots, 8, 128), F32),
            vmem((planes, proj // 128 + 8, 128), F32),
            vmem((1, proj), F32),
            sem((2,)),
            sem((slots,)),
            sem((slots,)),
            sem((slots,)),
            sem((slots,)),
            sem((2,)),
            sem((wide,)),
            sem((wide,)),
            sem((planes - 1,)),
            sem((planes - 1,)),
            sem((wide,)),
            sem((wide,)),
            sem((slots,)),
            sem((slots,)),
            sem((planes - 1,)),
            sem((planes - 1,)),
            sem((2 * slots,)),
            sem((2 * slots,)),
        ],
        compiler_params=pltpu.CompilerParams(
            collective_id=0, has_side_effects=True, vmem_limit_bytes=62 * 1024 * 1024
        ),
    )(module_slot, lengths, act_factors, grad_factors, query_grads[0])
    return result.T


def solution(mesh):
    planes = mesh.shape["dp"] // 2
    return jax.shard_map(
        functools.partial(per_device, planes),
        mesh=mesh,
        in_specs=(
            P(("dp", "module"), None, None, None),
            P(("dp", "module"), None, None, None),
            P(("dp", "module")),
            P(),
            P("module", "dp", None),
        ),
        out_specs=P("dp", "module"),
        check_vma=False,
    )
```

time: 854 us -> 124 us (0.15)
  waiting for transfers between devices: 624 us -> 0 us
  blocking collectives: 181 us -> 0 us
  Pallas kernels: 0 us -> 123 us
  matrix products: 19.9 us -> 0 us
  between operations: 14.9 us -> 0.01 us
    all_gather x4 -> x0, waiting for transfers between devices: 502 us -> none  [the longest x3 372 us: spread(): lax.all_gather(step, 'dp', axis=0, tiled=True)]
    psum x1 -> x0, blocking collectives: 124 us -> none  [per_device(): traces = lax.psum(own_slot * local_trace, ('dp', 'module'))]
    pallas_call x0 -> x1, Pallas kernels: none -> 123 us  [per_device(): pl.pallas_call(functools.partial(kernel, planes), out_shape=jax.ShapeDtyp...]
    reduce_scatter x1 -> x0, waiting for transfers between devices: 122 us -> none  [per_device(): lax.psum_scatter(lax.dot_general(columns, train, (((0,), (0,)), ((), ()))...]
    all_to_all x2 -> x0, blocking collectives: 57.4 us -> none  [the longest x1 36.9 us: per_device(): lax.all_to_all(partial_scores[None].astype(jnp.bfloat16), 'module', split...]
    dot_general x7 -> x0, matrix products: 19.9 us -> none  [the longest x3 10.7 us: spread(): jnp.dot(gram_rows, lax.all_gather(step, 'dp', axis=0, tiled=True), precis...]
  transfers between devices with their start and end apart: 5 -> 0, of which waited for: 5 -> 0; matrix products, arithmetic and copies ran while one was open for 0% -> 0% of each run, Pallas kernels for 0% -> 0%
where the time goes in v1:
time: 124 us
  Pallas kernels  123 us (99%)
  local copies, waits for them, and re-layouts  1.38 us (1%)
    pallas_call x1, Pallas kernels, per_device(): pl.pallas_call(functools.partial(kernel, planes), out_shape=jax.ShapeDtyp...  123 us

profile of v1, /device:TPU:1, one launch (start us, length us, event | category | flops | bytes accessed | tf_op | source)
XLA Modules:
  0.0 124.2 jit_solution(1189141948465861697)
XLA Ops:
  0.0 122.8 %shard_map.55 = f32[32,256]{1,0:T(8,128)} custom-call(s32[16]{0:T(128)} %slot_ref.1, s32[16]{0:T(128)} %len_ref.1, bf16[16,16,32,128]{3,2,1,0:T(8,128)(2,1)} %act_hbm.1, bf16[16,16,32,128]{3,2,1,0:T(8,128)(2,1)} %grad_hbm.1, f32[32,512]{1,0:T(8,128)} %bitcast.3), custom_call_target="tpu_custom_call" | custom-call | tf_op jit(solution)/shard_map/pallas_call | solution.py:514
  122.8 1.4 %copy.7 = f32[256,32]{0,1:T(8,128)} copy(f32[256,32]{0,1:T(8,128)} %bitcast.2) | data formatting | bytes 65536

commit v2 on v1

v2 whole, which is shorter than its diff:
```python
import functools

import jax
import jax.numpy as jnp
from jax import lax
from jax.experimental import pallas as pl
from jax.experimental.pallas import tpu as pltpu
from jax.sharding import PartitionSpec as P

ITERS = 4
NEAR = (2, -2, 1, -1)
FAR = 5
MESH = pl.DeviceIdType.MESH
BF16 = jnp.bfloat16
F32 = jnp.float32


def kernel(
    planes,
    slot_ref,
    len_ref,
    act_hbm,
    grad_hbm,
    query_ref,
    out_ref,
    act,
    grad,
    prod,
    tsend,
    tall,
    gpart,
    gcirc,
    gfull,
    gsend,
    near_in,
    far_out,
    far_in,
    qsrc,
    qfull,
    step_ref,
    resid_ref,
    acc_ref,
    ssend,
    srecv,
    slot_traces,
    plane_diags,
    diag_ref,
    load_sem,
    t_send,
    t_recv,
    tsib_send,
    tsib_recv,
    pair_send,
    pair_recv,
    q_send,
    q_recv,
    rs_send,
    rs_recv,
    g_send,
    g_recv,
    d_send,
    d_recv,
    tr_send,
    tr_recv,
    s_send,
    s_recv,
):
    per_dev, slots, rank, span = act.shape
    proj = rank * rank
    blocks = proj // 128
    kept = gcirc.shape[1]
    half = proj // 2
    band = half // planes
    rows = slots * per_dev
    queries = qfull.shape[1]
    per_owner = queries // slots
    assert planes == 16 and slots == 16
    examples = rows * 2 * planes

    dp, mod = lax.axis_index("dp"), lax.axis_index("module")
    z, y_lo = dp // 2, dp % 2
    core = mod % 2
    slot = (mod // 2) * 2 + y_lo

    def device(plane, chip, cc):
        return (plane * 2 + chip % 2, (chip // 2) * 2 + cc)

    way = 1 - 2 * core

    def along(count):
        return (z + 2 * planes + count) % planes

    def remote(src, dst, send, recv, target):
        return pltpu.make_async_remote_copy(
            src_ref=src, dst_ref=dst, send_sem=send, recv_sem=recv,
            device_id=target, device_id_type=MESH,
        )

    sibling = device(z, slot, 1 - core)

    def off(count):
        return device(along(count), slot, core)

    loads = [
        pltpu.make_async_copy(act_hbm, act, load_sem.at[0]),
        pltpu.make_async_copy(grad_hbm, grad, load_sem.at[1]),
    ]
    for load in loads:
        load.start()

    barrier = pltpu.get_barrier_semaphore()

    def greet(index, carry):
        chip, cc = index // 2, index % 2

        @pl.when(jnp.logical_or(chip != slot, cc != core))
        def _():
            pl.semaphore_signal(
                barrier, inc=1, device_id=device(z, chip, cc), device_id_type=MESH
            )

        return carry

    lax.fori_loop(0, 2 * slots, greet, 0)
    for count in NEAR + (3, -3, FAR, -FAR):
        pl.semaphore_signal(barrier, inc=1, device_id=off(count), device_id_type=MESH)
    qsrc[...] = query_ref[...].astype(BF16)

    for load in loads:
        load.wait()

    lanes = lax.broadcasted_iota(jnp.int32, (8, 4 * rank), 1) // rank
    positions = lax.broadcasted_iota(jnp.int32, (4 * rank, span), 1)

    def t_first(chip, cc):
        first = cc * rows + (chip % 2) * (rows // 2) + (chip // 2) * per_dev
        return pl.ds(pl.multiple_of(first, per_dev), per_dev)

    def t_rows(chip, cc):
        return tall.at[t_first(chip, cc), :]

    def holder(chip):
        found = jnp.int32(0)
        for index in range(slots):
            found = jnp.where(slot_ref[index] == chip, index, found)
        return found

    def project(first):
        held = [holder(first + r) for r in range(4)]
        for e in range(per_dev):
            left = jnp.concatenate([act[e, h] for h in held], axis=0)
            right = jnp.concatenate([grad[e, h] for h in held], axis=0)
            left = jnp.where(positions < len_ref[e], left, jnp.zeros_like(left))
            prod[pl.ds(e * 4 * rank, 4 * rank), :] = lax.dot_general(
                left, right, (((1,), (1,)), ((), ())), preferred_element_type=F32
            )
        for r in range(4):
            for g in range(proj // (4 * rank)):
                halves = []
                for h in range(per_dev // 8):
                    merged = None
                    for b in range(4):
                        row = h * 8 * 4 * rank + r * rank + 4 * g + b
                        piece = prod[pl.ds(row, 8, stride=4 * rank), :]
                        if b != r:
                            piece = pltpu.roll(piece, ((b - r) % 4) * rank, 1)
                        merged = piece if merged is None else jnp.where(lanes == b, piece, merged)
                    halves.append(merged)
                tsend[first + r, :, pl.ds(g * 4 * rank, 4 * rank)] = jnp.concatenate(
                    halves, axis=0
                ).astype(BF16)

    def t_to(chip):
        return remote(
            tsend.at[chip], t_rows(slot, core), t_send.at[chip], t_recv.at[slot],
            device(z, chip, core),
        )

    partner = device(z, (slot // 2) * 2 + core, y_lo)

    def q_part(plane):
        return qfull.at[pl.ds(pl.multiple_of((plane * 2 + core) * band, band), band), :]

    dp_rows = pl.ds(pl.multiple_of(dp * band, band), band)
    pair_out = remote(qsrc, qfull.at[dp_rows, :], pair_send.at[0], pair_recv.at[0], partner)
    pair_in = remote(q_part(z), q_part(z), pair_send.at[0], pair_recv.at[0], partner)

    def gather(part, send, recv, share):
        def carried(offset, count):
            block = part(along(offset))
            mark = (offset - count) % planes
            return remote(block, block, send.at[mark], recv.at[mark], off(count))

        def arrived(mark):
            block = part(along(mark))
            return remote(block, block, send.at[mark], recv.at[mark], sibling)

        def last():
            block = part(along(FAR * way))
            return remote(block, block, send.at[8], recv.at[8], off(-3 * way))

        def across(mark):
            block = part(along(mark))
            return remote(
                block, block, send.at[planes + mark], recv.at[planes + mark], sibling
            )

        def begin():
            for count in (FAR, -FAR) + NEAR:
                carried(0, count).start()
            if share:
                across(0).start()

        def go_on():
            for offset in (FAR, -FAR):
                arrived(offset % planes).wait_recv()
                for count in NEAR:
                    carried(offset, count).start()
            last().start()
            if share:
                across(FAR).start()
                across(planes - FAR).start()

        def finish():
            rest = [n % planes for n in (1, -1, 2, -2, 6, -6, 4, -4, 7, -7, 3, -3, 8)]
            for mark in rest:
                arrived(mark).wait_recv()
                if share:
                    across(mark).start()
            if share:
                for mark in [0, FAR, planes - FAR] + rest:
                    other = remote(
                        share(along(mark)), share(along(mark)), send.at[planes + mark],
                        recv.at[planes + mark], sibling,
                    )
                    other.wait_recv()
                    across(mark).wait_send()
            for count in (FAR, -FAR) + NEAR:
                carried(0, count).wait_send()
            for offset in (FAR, -FAR):
                for count in NEAR:
                    carried(offset, count).wait_send()
            last().wait_send()

        return begin, go_on, finish

    q_begin, q_go_on, q_finish = gather(
        q_part, q_send, q_recv,
        lambda plane: qfull.at[
            pl.ds(pl.multiple_of((plane * 2 + 1 - core) * band, band), band), :
        ],
    )
    d_begin, d_go_on, d_finish = gather(lambda plane: plane_diags.at[plane], d_send, d_recv, None)
    g_begin, g_go_on, g_finish = gather(
        lambda plane: gcirc.at[pl.ds(pl.multiple_of(core * half + plane * band, band), band), :],
        g_send, g_recv,
        lambda plane: gcirc.at[
            pl.ds(pl.multiple_of((1 - core) * half + plane * band, band), band), :
        ],
    )

    def first_of(k):
        return ((slot // 4 + 1 + k) % (slots // 4)) * 4

    def scatter(first):
        for r in range(4):

            @pl.when(first + r != slot)
            def _():
                t_to(first + r).start()

    project(first_of(0))
    pl.semaphore_wait(barrier, 2 * slots - 1 + 8)

    @pl.when(y_lo != core)
    def _():
        pair_out.start()

    @pl.when(y_lo == core)
    def _():
        qfull[dp_rows, :] = qsrc[...]

    scatter(first_of(0))

    def group(k, carry):
        project(first_of(k))
        scatter(first_of(k))

        @pl.when(k == 1)
        def _():
            pl.when(y_lo != core)(lambda: pair_in.wait_recv())
            q_begin()

        return carry

    lax.fori_loop(1, slots // 4, group, 0)
    tall[t_first(slot, core), :] = tsend[slot]

    def collect(k, carry):
        chip = ((slot // 4 + slots // 4 - 1 - k // 4) % (slots // 4)) * 4 + (slot + k) % 4

        @pl.when(chip != slot)
        def _():
            remote(
                t_rows(chip, core), t_rows(chip, core), t_send.at[chip], t_recv.at[chip], sibling
            ).wait_recv()

        remote(
            t_rows(chip, core), t_rows(chip, core), tsib_send.at[chip], tsib_recv.at[chip], sibling
        ).start()
        return carry

    lax.fori_loop(0, slots // 2, collect, 0)
    q_go_on()
    lax.fori_loop(slots // 2, slots, collect, 0)

    def collected(chip, carry):
        other = remote(
            t_rows(chip, 1 - core), t_rows(chip, 1 - core), tsib_send.at[chip], tsib_recv.at[chip],
            sibling,
        )
        other.wait_recv()
        other.wait_send()
        return carry

    lax.fori_loop(0, slots, collected, 0)

    apart = lax.broadcasted_iota(jnp.int32, (128, 128), 0) != lax.broadcasted_iota(
        jnp.int32, (128, 128), 1
    )
    per_block = 128 // band

    def columns(start, count):
        return tall[:, pl.ds(pl.multiple_of(start, 128), count)]

    def store(n, offset, value):
        for q in range(per_block):
            piece = value[q * band : (q + 1) * band]
            gpart[n * per_block + q, :, pl.ds(offset, value.shape[1])] = piece
            gsend[n * per_block + q, :, pl.ds(offset, value.shape[1])] = piece.astype(BF16)

    for n in range(half // 128):
        first = core * half + n * 128
        left = columns(first, 128)
        direct = half - n * 128
        value = lax.dot_general(
            left, columns(first, direct), (((0,), (0,)), ((), ())), preferred_element_type=F32
        )
        store(n, 0, jnp.where(apart, value[:, :128], 0.0))
        if direct > 128:
            store(n, 128, value[:, 128:])
        value = lax.dot_general(
            left, columns((1 - core) * half, kept - direct), (((0,), (0,)), ((), ())),
            preferred_element_type=F32,
        )
        store(n, direct, value)

    def near_send(count, a):
        index = NEAR.index(count) * 3 + a + 1
        return remote(
            gsend.at[along(count - FAR * a)], near_in.at[index], rs_send.at[index],
            rs_recv.at[index], off(count),
        )

    extra = 3 * len(NEAR)
    last_send = remote(
        gsend.at[along(8)], near_in.at[extra], rs_send.at[extra], rs_recv.at[extra], off(-3 * way)
    )

    def far_send(a):
        index = extra + 1 + (a + 1) // 2
        return remote(
            far_out.at[(a + 1) // 2], far_in.at[(a + 1) // 2], rs_send.at[index],
            rs_recv.at[index], off(-FAR * a),
        )

    for count in NEAR:
        for a in (1, -1):
            near_send(count, a).start()
    last_send.start()
    for count in NEAR:
        near_send(count, 0).start()

    squares = tall[...].astype(F32)
    squares = jnp.sum(squares * squares, axis=0, keepdims=True)
    for n in range(blocks):
        plane_diags[z, pl.ds(n, 1), :] = squares[:, n * 128 : (n + 1) * 128]
    d_begin()

    def window(a):
        value = gpart[along(-FAR * a)]
        for count in NEAR:
            near_send(count, a).wait_recv()
            value = value + near_in[NEAR.index(count) * 3 + a + 1].astype(F32)
        return value

    upward, downward = window(1), window(-1)
    last_send.wait_recv()
    more = near_in[extra].astype(F32)
    far_out[1] = (upward + jnp.where(core == 0, more, 0.0)).astype(BF16)
    far_send(1).start()
    far_out[0] = (downward + jnp.where(core == 0, 0.0, more)).astype(BF16)
    far_send(-1).start()
    d_go_on()
    value = window(0)
    d_finish()

    diagonal = jnp.sum(plane_diags[...], axis=0) / examples
    own_eig = jnp.sum(jnp.sum(diagonal, axis=1, keepdims=True), axis=0, keepdims=True) / proj
    slot_traces[slot] = jnp.broadcast_to(own_eig, (8, 128))
    diag_ref[...] = jnp.concatenate([diagonal[n : n + 1] for n in range(blocks)], axis=1)

    def trace_to(chip):
        return remote(
            slot_traces.at[slot], slot_traces.at[slot], tr_send.at[chip], tr_recv.at[slot],
            device(z, chip, core),
        )

    def trace_from(chip):
        return remote(
            slot_traces.at[chip], slot_traces.at[chip], tr_send.at[chip], tr_recv.at[chip], sibling
        )

    def tell(k, carry):
        trace_to((slot + k) % slots).start()
        return carry

    for a in (1, -1):
        far_send(a).wait_recv()
        value = value + far_in[(a + 1) // 2].astype(F32)
    gcirc[pl.ds(pl.multiple_of(core * half + z * band, band), band), :] = value.astype(BF16)
    g_begin()
    lax.fori_loop(1, slots, tell, 0)

    def settle(k, carry):
        chip = (slot + k) % slots
        t_to(chip).wait_send()
        trace_to(chip).wait_send()
        trace_from(chip).wait_recv()
        return carry

    lax.fori_loop(1, slots, settle, 0)
    pl.when(y_lo != core)(lambda: pair_out.wait_send())
    for count in NEAR:
        for a in (1, -1, 0):
            near_send(count, a).wait_send()
    last_send.wait_send()
    for a in (1, -1):
        far_send(a).wait_send()
    g_go_on()
    q_finish()
    g_finish()

    for n in range(blocks):
        for k in range(kept // 128):
            piece = gcirc[n * 128 : (n + 1) * 128, k * 128 : (k + 1) * 128]
            other = (n + k) % blocks
            gfull[n * 128 : (n + 1) * 128, other * 128 : (other + 1) * 128] = piece
            if 0 < k < blocks - k:
                gfull[other * 128 : (other + 1) * 128, n * 128 : (n + 1) * 128] = piece.T

    damping = 0.1 * (jnp.sum(slot_traces[...], axis=0)[0:1, 0:1] / slots)
    upper = damping + 4.0 * own_eig
    center = (upper + damping) / 2.0
    radius = (upper - damping) / 2.0
    sigma = center / radius
    rho = 1.0 / sigma
    train = tall[pl.ds(pl.multiple_of(core * rows, rows), rows), :].astype(F32)
    resid_ref[...] = train
    step_ref[...] = train / center
    acc_ref[...] = step_ref[...]
    tile = min(256, proj)
    for index in range(ITERS - 1):
        rho_next = 1.0 / (2.0 * sigma - rho)
        rounded = step_ref[...].astype(BF16)

        def column(n, carry):
            cols = pl.ds(pl.multiple_of(n * tile, tile), tile)
            product = jnp.dot(rounded, gfull[:, cols], preferred_element_type=F32)
            step = step_ref[:, cols]
            resid = resid_ref[:, cols] - (
                product * (1.0 / examples) + (diag_ref[:, cols] + damping) * step
            )
            resid_ref[:, cols] = resid
            step = rho_next * rho * step + (2.0 * rho_next / radius) * resid
            step_ref[:, cols] = step
            acc_ref[:, cols] = acc_ref[:, cols] + step
            return carry

        lax.fori_loop(0, proj // tile, column, 0)
        rho = rho_next

    scores = jnp.dot(acc_ref[...].astype(BF16), qfull[...], preferred_element_type=F32)
    ssend[...] = scores.T.astype(BF16)

    def block(index):
        owner, low = index // 2, index % 2
        return ssend.at[
            pl.ds(pl.multiple_of(owner * per_owner, per_owner), per_owner),
            pl.ds(pl.multiple_of(low * (rows // 2), rows // 2), rows // 2),
        ]

    mark = slot * 2 + core

    def score_to(index):
        return remote(
            block(index), srecv.at[mark], s_send.at[index], s_recv.at[mark],
            (z * 2 + index % 2, index // 2),
        )

    own = mod * 2 + y_lo

    def push(k, carry):
        index = (own + k) % (2 * slots)
        score_to(index).start()
        return carry

    lax.fori_loop(1, 2 * slots, push, 0)
    srecv[mark] = ssend[
        pl.ds(pl.multiple_of(mod * per_owner, per_owner), per_owner),
        pl.ds(pl.multiple_of(y_lo * (rows // 2), rows // 2), rows // 2),
    ]

    def pull(k, carry):
        index = (mark + k) % (2 * slots)
        remote(
            srecv.at[index], srecv.at[index], s_send.at[index], s_recv.at[index], sibling
        ).wait_recv()
        return carry

    lax.fori_loop(1, 2 * slots, pull, 0)
    sums = []
    for cc in range(2):
        summed = srecv[cc].astype(F32)
        for chip in range(1, slots):
            summed = summed + srecv[chip * 2 + cc].astype(F32)
        sums.append(summed)
    width = rows // 2
    runs = width // per_dev
    lane_run = lax.broadcasted_iota(jnp.int32, (per_owner, width), 1) // per_dev
    for h in range(2):
        merged = jnp.zeros((per_owner, width), F32)
        for n in range(runs // 2):
            for cc in range(2):
                shift = (2 * n + cc - (h * (runs // 2) + n)) % runs
                piece = pltpu.roll(sums[cc], shift * per_dev, 1) if shift else sums[cc]
                merged = jnp.where(lane_run == 2 * n + cc, piece, merged)
        out_ref[:, pl.ds(h * width, width)] = merged

    def pushed(k, carry):
        score_to((own + k) % (2 * slots)).wait_send()
        return carry

    lax.fori_loop(1, 2 * slots, pushed, 0)


def per_device(planes, act_factors, grad_factors, lengths, module_slot, query_grads):
    per_dev, slots, rank, span = act_factors.shape
    proj = rank * rank
    rows = slots * per_dev
    band, queries = query_grads.shape[1:]
    per_owner = queries // slots
    kept = (proj // 128 // 2 + 1) * 128
    sem = pltpu.SemaphoreType.DMA
    vmem = pltpu.VMEM
    result = pl.pallas_call(
        functools.partial(kernel, planes),
        out_shape=jax.ShapeDtypeStruct((per_owner, rows), F32),
        in_specs=[
            pl.BlockSpec(memory_space=pltpu.SMEM),
            pl.BlockSpec(memory_space=pltpu.SMEM),
            pl.BlockSpec(memory_space=pltpu.HBM),
            pl.BlockSpec(memory_space=pltpu.HBM),
            pl.BlockSpec(memory_space=pltpu.VMEM),
        ],
        out_specs=pl.BlockSpec(memory_space=pltpu.VMEM),
        scratch_shapes=[
            vmem((per_dev, slots, rank, span), BF16),
            vmem((per_dev, slots, rank, span), BF16),
            vmem((per_dev * 4 * rank, 4 * rank), F32),
            vmem((slots, per_dev, proj), BF16),
            vmem((2 * rows, proj), BF16),
            vmem((planes, band, kept), F32),
            vmem((proj, kept), BF16),
            vmem((proj, proj), BF16),
            vmem((planes, band, kept), BF16),
            vmem((13, band, kept), BF16),
            vmem((2, band, kept), BF16),
            vmem((2, band, kept), BF16),
            vmem((band, queries), BF16),
            vmem((proj, queries), BF16),
            vmem((rows, proj), F32),
            vmem((rows, proj), F32),
            vmem((rows, proj), F32),
            vmem((queries, rows), BF16),
            vmem((2 * slots, per_owner, rows // 2), BF16),
            vmem((slots, 8, 128), F32),
            vmem((planes, proj // 128, 128), F32),
            vmem((1, proj), F32),
            sem((2,)),
            sem((slots,)),
            sem((slots,)),
            sem((slots,)),
            sem((slots,)),
            sem((1,)),
            sem((1,)),
            sem((2 * planes,)),
            sem((2 * planes,)),
            sem((15,)),
            sem((15,)),
            sem((2 * planes,)),
            sem((2 * planes,)),
            sem((planes,)),
            sem((planes,)),
            sem((slots,)),
            sem((slots,)),
            sem((2 * slots,)),
            sem((2 * slots,)),
        ],
        compiler_params=pltpu.CompilerParams(
            collective_id=0, has_side_effects=True, vmem_limit_bytes=62 * 1024 * 1024
        ),
    )(module_slot, lengths, act_factors, grad_factors, query_grads[0])
    return result.T


def solution(mesh):
    planes = mesh.shape["dp"] // 2
    return jax.shard_map(
        functools.partial(per_device, planes),
        mesh=mesh,
        in_specs=(
            P(("dp", "module"), None, None, None),
            P(("dp", "module"), None, None, None),
            P(("dp", "module")),
            P(),
            P("module", "dp", None),
        ),
        out_specs=P("dp", "module"),
        check_vma=False,
    )
```

time: 124 us -> 87.9 us (0.71)
  Pallas kernels: 123 us -> 86.3 us
    pallas_call x1, Pallas kernels: 123 us -> 86.3 us  [per_device(): pl.pallas_call(functools.partial(kernel, planes), out_shape=jax.ShapeDtyp...]
where the time goes in v2:
time: 87.9 us; the launch traced here: 87.7 us
  Pallas kernels  86.3 us (98%)
  local copies, waits for them, and re-layouts  1.38 us (2%)
    pallas_call x1, Pallas kernels, per_device(): pl.pallas_call(functools.partial(kernel, planes), out_shape=jax.ShapeDtyp...  86.3 us

profile of v2, /device:TPU:1, one launch (start us, length us, event | category | flops | bytes accessed | tf_op | source)
XLA Modules:
  0.0 87.7 jit_solution(2760191620302890930)
XLA Ops:
  0.0 86.3 %shard_map.55 = f32[32,256]{1,0:T(8,128)} custom-call(s32[16]{0:T(128)} %slot_ref.1, s32[16]{0:T(128)} %len_ref.1, bf16[16,16,32,128]{3,2,1,0:T(8,128)(2,1)} %act_hbm.1, bf16[16,16,32,128]{3,2,1,0:T(8,128)(2,1)} %grad_hbm.1, f32[32,512]{1,0:T(8,128)} %bitcast.3), custom_call_target="tpu_custom_call" | custom-call | tf_op jit(solution)/shard_map/pallas_call | solution.py:566
  86.3 1.4 %copy.7 = f32[256,32]{0,1:T(8,128)} copy(f32[256,32]{0,1:T(8,128)} %bitcast.2) | data formatting | bytes 65536

commit v3 on v2

--- a/solution.py
+++ b/solution.py
@@ -10,6 +10,7 @@
 ITERS = 4
 NEAR = (2, -2, 1, -1)
 FAR = 5
+LOADS = 4
 MESH = pl.DeviceIdType.MESH
 BF16 = jnp.bfloat16
 F32 = jnp.float32
@@ -50,8 +51,6 @@
     t_recv,
     tsib_send,
     tsib_recv,
-    pair_send,
-    pair_recv,
     q_send,
     q_recv,
     rs_send,
@@ -101,14 +100,14 @@
     def off(count):
         return device(along(count), slot, core)
 
-    loads = [
-        pltpu.make_async_copy(act_hbm, act, load_sem.at[0]),
-        pltpu.make_async_copy(grad_hbm, grad, load_sem.at[1]),
-    ]
-    for load in loads:
-        load.start()
+    def twin(count):
+        return device(along(count), (slot // 2) * 2 + core, y_lo)
 
     barrier = pltpu.get_barrier_semaphore()
+    for count in (FAR, -FAR, 3, -3) + NEAR:
+        pl.semaphore_signal(barrier, inc=1, device_id=off(count), device_id_type=MESH)
+    for count in (FAR, -FAR) + NEAR:
+        pl.semaphore_signal(barrier, inc=1, device_id=twin(count), device_id_type=MESH)
 
     def greet(index, carry):
         chip, cc = index // 2, index % 2
@@ -122,8 +121,17 @@
         return carry
 
     lax.fori_loop(0, 2 * slots, greet, 0)
-    for count in NEAR + (3, -3, FAR, -FAR):
-        pl.semaphore_signal(barrier, inc=1, device_id=off(count), device_id_type=MESH)
+    part = per_dev // LOADS
+    loads = [
+        pltpu.make_async_copy(
+            whole.at[pl.ds(n * part, part)], held.at[pl.ds(n * part, part)], load_sem.at[n, side]
+        )
+        for n in range(LOADS)
+        for side, (whole, held) in enumerate(((act_hbm, act), (grad_hbm, grad)))
+    ]
+    for load in loads:
+        load.start()
+
     qsrc[...] = query_ref[...].astype(BF16)
 
     for load in loads:
@@ -145,13 +153,15 @@
             found = jnp.where(slot_ref[index] == chip, index, found)
         return found
 
-    def project(first):
-        held = [holder(first + r) for r in range(4)]
+    pitch = prod.shape[0] // per_dev
+
+    def project(chips):
+        held = [holder(chip) for chip in chips]
         for e in range(per_dev):
             left = jnp.concatenate([act[e, h] for h in held], axis=0)
             right = jnp.concatenate([grad[e, h] for h in held], axis=0)
             left = jnp.where(positions < len_ref[e], left, jnp.zeros_like(left))
-            prod[pl.ds(e * 4 * rank, 4 * rank), :] = lax.dot_general(
+            prod[pl.ds(e * pitch, 4 * rank), :] = lax.dot_general(
                 left, right, (((1,), (1,)), ((), ())), preferred_element_type=F32
             )
         for r in range(4):
@@ -160,13 +170,13 @@
                 for h in range(per_dev // 8):
                     merged = None
                     for b in range(4):
-                        row = h * 8 * 4 * rank + r * rank + 4 * g + b
-                        piece = prod[pl.ds(row, 8, stride=4 * rank), :]
+                        row = h * 8 * pitch + r * rank + 4 * g + b
+                        piece = prod[pl.ds(row, 8, stride=pitch), :]
                         if b != r:
                             piece = pltpu.roll(piece, ((b - r) % 4) * rank, 1)
                         merged = piece if merged is None else jnp.where(lanes == b, piece, merged)
                     halves.append(merged)
-                tsend[first + r, :, pl.ds(g * 4 * rank, 4 * rank)] = jnp.concatenate(
+                tsend[chips[r], :, pl.ds(g * 4 * rank, 4 * rank)] = jnp.concatenate(
                     halves, axis=0
                 ).astype(BF16)
 
@@ -176,14 +186,16 @@
             device(z, chip, core),
         )
 
-    partner = device(z, (slot // 2) * 2 + core, y_lo)
-
     def q_part(plane):
         return qfull.at[pl.ds(pl.multiple_of((plane * 2 + core) * band, band), band), :]
 
     dp_rows = pl.ds(pl.multiple_of(dp * band, band), band)
-    pair_out = remote(qsrc, qfull.at[dp_rows, :], pair_send.at[0], pair_recv.at[0], partner)
-    pair_in = remote(q_part(z), q_part(z), pair_send.at[0], pair_recv.at[0], partner)
+
+    def q_first(count):
+        mark = -count % planes
+        return remote(qsrc, qfull.at[dp_rows, :], q_send.at[mark], q_recv.at[mark], twin(count))
+
+    q_home = remote(q_part(z), q_part(z), q_send.at[0], q_recv.at[0], sibling)
 
     def gather(part, send, recv, share):
         def carried(offset, count):
@@ -208,8 +220,6 @@
         def begin():
             for count in (FAR, -FAR) + NEAR:
                 carried(0, count).start()
-            if share:
-                across(0).start()
 
         def go_on():
             for offset in (FAR, -FAR):
@@ -218,8 +228,8 @@
                     carried(offset, count).start()
             last().start()
             if share:
-                across(FAR).start()
-                across(planes - FAR).start()
+                for mark in (0, FAR, planes - FAR):
+                    across(mark).start()
 
         def finish():
             rest = [n % planes for n in (1, -1, 2, -2, 6, -6, 4, -4, 7, -7, 3, -3, 8)]
@@ -244,7 +254,7 @@
 
         return begin, go_on, finish
 
-    q_begin, q_go_on, q_finish = gather(
+    _, q_go_on, q_finish = gather(
         q_part, q_send, q_recv,
         lambda plane: qfull.at[
             pl.ds(pl.multiple_of((plane * 2 + 1 - core) * band, band), band), :
@@ -259,60 +269,67 @@
         ],
     )
 
-    def first_of(k):
-        return ((slot // 4 + 1 + k) % (slots // 4)) * 4
-
-    def scatter(first):
+    def chips_of(k, sign):
+        chips = []
         for r in range(4):
-
-            @pl.when(first + r != slot)
+            x, y = (slot // 4 + 4 + sign * r) % 4, (slot + 4 + sign * ((r + k) % 4)) % 4
+            chips.append(x * 4 + y)
+        return chips
+
+    def scatter(chips):
+        for r in (2, 1, 3, 0):
+
+            @pl.when(chips[r] != slot)
             def _():
-                t_to(first + r).start()
-
-    project(first_of(0))
-    pl.semaphore_wait(barrier, 2 * slots - 1 + 8)
+                t_to(chips[r]).start()
+
+    def group(k, carry):
+        project(chips_of(k, 1))
+        return carry
+
+    lax.fori_loop(1, slots // 4 + 1, group, 0)
+    pl.semaphore_wait(barrier, 2 * slots - 1 + 14)
+
+    def spread(k, carry):
+        scatter(chips_of(k, 1))
+        return carry
+
+    lax.fori_loop(1, slots // 4 + 1, spread, 0)
+    for count in (FAR, -FAR) + NEAR:
+        q_first(count).start()
 
     @pl.when(y_lo != core)
     def _():
-        pair_out.start()
+        q_first(0).start()
 
     @pl.when(y_lo == core)
     def _():
         qfull[dp_rows, :] = qsrc[...]
 
-    scatter(first_of(0))
-
-    def group(k, carry):
-        project(first_of(k))
-        scatter(first_of(k))
-
-        @pl.when(k == 1)
-        def _():
-            pl.when(y_lo != core)(lambda: pair_in.wait_recv())
-            q_begin()
-
-        return carry
-
-    lax.fori_loop(1, slots // 4, group, 0)
     tall[t_first(slot, core), :] = tsend[slot]
 
     def collect(k, carry):
-        chip = ((slot // 4 + slots // 4 - 1 - k // 4) % (slots // 4)) * 4 + (slot + k) % 4
-
-        @pl.when(chip != slot)
-        def _():
+        chips = chips_of(k, -1)
+        for r in (1, 3, 2, 0):
+            chip = chips[r]
+
+            @pl.when(chip != slot)
+            def _():
+                remote(
+                    t_rows(chip, core), t_rows(chip, core), t_send.at[chip], t_recv.at[chip],
+                    sibling,
+                ).wait_recv()
+
             remote(
-                t_rows(chip, core), t_rows(chip, core), t_send.at[chip], t_recv.at[chip], sibling
-            ).wait_recv()
-
-        remote(
-            t_rows(chip, core), t_rows(chip, core), tsib_send.at[chip], tsib_recv.at[chip], sibling
-        ).start()
-        return carry
-
-    lax.fori_loop(0, slots // 2, collect, 0)
+                t_rows(chip, core), t_rows(chip, core), tsib_send.at[chip], tsib_recv.at[chip],
+                sibling,
+            ).start()
+        return carry
+
+    lax.fori_loop(1, 3, collect, 0)
+    pl.when(y_lo != core)(lambda: q_home.wait_recv())
     q_go_on()
-    lax.fori_loop(slots // 2, slots, collect, 0)
+    lax.fori_loop(3, slots // 4 + 1, collect, 0)
 
     def collected(chip, carry):
         other = remote(
@@ -378,8 +395,6 @@
         for a in (1, -1):
             near_send(count, a).start()
     last_send.start()
-    for count in NEAR:
-        near_send(count, 0).start()
 
     squares = tall[...].astype(F32)
     squares = jnp.sum(squares * squares, axis=0, keepdims=True)
@@ -401,36 +416,40 @@
     far_send(1).start()
     far_out[0] = (downward + jnp.where(core == 0, 0.0, more)).astype(BF16)
     far_send(-1).start()
+    for count in NEAR:
+        near_send(count, 0).start()
     d_go_on()
     value = window(0)
-    d_finish()
-
-    diagonal = jnp.sum(plane_diags[...], axis=0) / examples
-    own_eig = jnp.sum(jnp.sum(diagonal, axis=1, keepdims=True), axis=0, keepdims=True) / proj
-    slot_traces[slot] = jnp.broadcast_to(own_eig, (8, 128))
-    diag_ref[...] = jnp.concatenate([diagonal[n : n + 1] for n in range(blocks)], axis=1)
-
-    def trace_to(chip):
-        return remote(
-            slot_traces.at[slot], slot_traces.at[slot], tr_send.at[chip], tr_recv.at[slot],
-            device(z, chip, core),
-        )
-
-    def trace_from(chip):
-        return remote(
-            slot_traces.at[chip], slot_traces.at[chip], tr_send.at[chip], tr_recv.at[chip], sibling
-        )
-
-    def tell(k, carry):
-        trace_to((slot + k) % slots).start()
-        return carry
 
     for a in (1, -1):
         far_send(a).wait_recv()
         value = value + far_in[(a + 1) // 2].astype(F32)
     gcirc[pl.ds(pl.multiple_of(core * half + z * band, band), band), :] = value.astype(BF16)
     g_begin()
+
+    d_finish()
+    diagonal = jnp.sum(plane_diags[...], axis=0) / examples
+    own_eig = jnp.sum(jnp.sum(diagonal, axis=1, keepdims=True), axis=0, keepdims=True) / proj
+    slot_traces[slot] = jnp.broadcast_to(own_eig, (8, 128))
+    diag_ref[...] = jnp.concatenate([diagonal[n : n + 1] for n in range(blocks)], axis=1)
+
+    def trace_to(chip):
+        return remote(
+            slot_traces.at[slot], slot_traces.at[slot], tr_send.at[chip], tr_recv.at[slot],
+            device(z, chip, core),
+        )
+
+    def trace_from(chip):
+        return remote(
+            slot_traces.at[chip], slot_traces.at[chip], tr_send.at[chip], tr_recv.at[chip], sibling
+        )
+
+    def tell(k, carry):
+        trace_to((slot + k) % slots).start()
+        return carry
+
     lax.fori_loop(1, slots, tell, 0)
+    g_go_on()
 
     def settle(k, carry):
         chip = (slot + k) % slots
@@ -440,14 +459,13 @@
         return carry
 
     lax.fori_loop(1, slots, settle, 0)
-    pl.when(y_lo != core)(lambda: pair_out.wait_send())
+    pl.when(y_lo != core)(lambda: q_first(0).wait_send())
     for count in NEAR:
         for a in (1, -1, 0):
             near_send(count, a).wait_send()
     last_send.wait_send()
     for a in (1, -1):
         far_send(a).wait_send()
-    g_go_on()
     q_finish()
     g_finish()
 
@@ -474,8 +492,8 @@
         rho_next = 1.0 / (2.0 * sigma - rho)
         rounded = step_ref[...].astype(BF16)
 
-        def column(n, carry):
-            cols = pl.ds(pl.multiple_of(n * tile, tile), tile)
+        for n in range(proj // tile):
+            cols = pl.ds(n * tile, tile)
             product = jnp.dot(rounded, gfull[:, cols], preferred_element_type=F32)
             step = step_ref[:, cols]
             resid = resid_ref[:, cols] - (
@@ -485,9 +503,6 @@
             step = rho_next * rho * step + (2.0 * rho_next / radius) * resid
             step_ref[:, cols] = step
             acc_ref[:, cols] = acc_ref[:, cols] + step
-            return carry
-
-        lax.fori_loop(0, proj // tile, column, 0)
         rho = rho_next
 
     scores = jnp.dot(acc_ref[...].astype(BF16), qfull[...], preferred_element_type=F32)
@@ -577,7 +592,7 @@
         scratch_shapes=[
             vmem((per_dev, slots, rank, span), BF16),
             vmem((per_dev, slots, rank, span), BF16),
-            vmem((per_dev * 4 * rank, 4 * rank), F32),
+            vmem((per_dev * (4 * rank + 8), 4 * rank), F32),
             vmem((slots, per_dev, proj), BF16),
             vmem((2 * rows, proj), BF16),
             vmem((planes, band, kept), F32),
@@ -597,13 +612,11 @@
             vmem((slots, 8, 128), F32),
             vmem((planes, proj // 128, 128), F32),
             vmem((1, proj), F32),
-            sem((2,)),
+            sem((LOADS, 2)),
             sem((slots,)),
             sem((slots,)),
             sem((slots,)),
             sem((slots,)),
-            sem((1,)),
-            sem((1,)),
             sem((2 * planes,)),
             sem((2 * planes,)),
             sem((15,)),

time: 87.9 us -> 85.3 us (0.970)
  Pallas kernels: 86.3 us -> 83.7 us
    pallas_call x1, Pallas kernels: 86.3 us -> 83.7 us  [per_device(): pl.pallas_call(functools.partial(kernel, planes), out_shape=jax.ShapeDtyp...]
where the time goes in v3:
time: 85.3 us; the launch traced here: 85 us
  Pallas kernels  83.7 us (98%)
  local copies, waits for them, and re-layouts  1.38 us (2%)
    pallas_call x1, Pallas kernels, per_device(): pl.pallas_call(functools.partial(kernel, planes), out_shape=jax.ShapeDtyp...  83.7 us

profile of v3, /device:TPU:1, one launch (start us, length us, event | category | flops | bytes accessed | tf_op | source)
XLA Modules:
  0.0 85.0 jit_solution(1323913956356854008)
XLA Ops:
  0.0 83.7 %shard_map.55 = f32[32,256]{1,0:T(8,128)} custom-call(s32[16]{0:T(128)} %slot_ref.1, s32[16]{0:T(128)} %len_ref.1, bf16[16,16,32,128]{3,2,1,0:T(8,128)(2,1)} %act_hbm.1, bf16[16,16,32,128]{3,2,1,0:T(8,128)(2,1)} %grad_hbm.1, f32[32,512]{1,0:T(8,128)} %bitcast.3), custom_call_target="tpu_custom_call" | custom-call | tf_op jit(solution)/shard_map/pallas_call | solution.py:581
  83.7 1.4 %copy.7 = f32[256,32]{0,1:T(8,128)} copy(f32[256,32]{0,1:T(8,128)} %bitcast.2) | data formatting | bytes 65536

commit v4 on v3

--- a/solution.py
+++ b/solution.py
@@ -197,77 +197,93 @@
 
     q_home = remote(q_part(z), q_part(z), q_send.at[0], q_recv.at[0], sibling)
 
-    def gather(part, send, recv, share):
-        def carried(offset, count):
-            block = part(along(offset))
+    def sized(act_on, cc):
+        pl.when(cc == 0)(lambda: act_on(kept))
+        pl.when(cc == 1)(lambda: act_on(kept - 128))
+
+    def gather(part, send, recv, share, run):
+        def carried(offset, count, width):
+            block = part(along(offset), width)
             mark = (offset - count) % planes
             return remote(block, block, send.at[mark], recv.at[mark], off(count))
 
-        def arrived(mark):
-            block = part(along(mark))
+        def arrived(mark, width):
+            block = part(along(mark), width)
             return remote(block, block, send.at[mark], recv.at[mark], sibling)
 
-        def last():
-            block = part(along(FAR * way))
+        def last(width):
+            block = part(along(FAR * way), width)
             return remote(block, block, send.at[8], recv.at[8], off(-3 * way))
 
-        def across(mark):
-            block = part(along(mark))
+        def across(mark, width):
+            block = part(along(mark), width)
             return remote(
                 block, block, send.at[planes + mark], recv.at[planes + mark], sibling
             )
 
-        def begin():
+        rest = [n % planes for n in (1, -1, 2, -2, 6, -6, 4, -4, 7, -7, 3, -3, 8)]
+
+        def begin(width):
             for count in (FAR, -FAR) + NEAR:
-                carried(0, count).start()
-
-        def go_on():
+                carried(0, count, width).start()
+
+        def go_on(width):
             for offset in (FAR, -FAR):
-                arrived(offset % planes).wait_recv()
+                arrived(offset % planes, width).wait_recv()
                 for count in NEAR:
-                    carried(offset, count).start()
-            last().start()
+                    carried(offset, count, width).start()
+            last(width).start()
             if share:
                 for mark in (0, FAR, planes - FAR):
-                    across(mark).start()
-
-        def finish():
-            rest = [n % planes for n in (1, -1, 2, -2, 6, -6, 4, -4, 7, -7, 3, -3, 8)]
+                    across(mark, width).start()
+
+        def finish(width):
             for mark in rest:
-                arrived(mark).wait_recv()
+                arrived(mark, width).wait_recv()
                 if share:
-                    across(mark).start()
+                    across(mark, width).start()
             if share:
                 for mark in [0, FAR, planes - FAR] + rest:
-                    other = remote(
-                        share(along(mark)), share(along(mark)), send.at[planes + mark],
-                        recv.at[planes + mark], sibling,
-                    )
-                    other.wait_recv()
-                    across(mark).wait_send()
+                    across(mark, width).wait_send()
             for count in (FAR, -FAR) + NEAR:
-                carried(0, count).wait_send()
+                carried(0, count, width).wait_send()
             for offset in (FAR, -FAR):
                 for count in NEAR:
-                    carried(offset, count).wait_send()
-            last().wait_send()
-
-        return begin, go_on, finish
+                    carried(offset, count, width).wait_send()
+            last(width).wait_send()
+
+        def shared(width):
+            for mark in [0, FAR, planes - FAR] + rest:
+                block = share(along(mark), width)
+                remote(
+                    block, block, send.at[planes + mark], recv.at[planes + mark], sibling
+                ).wait_recv()
+
+        def finish_all():
+            run(finish, core)
+            if share:
+                run(shared, 1 - core)
+
+        return lambda: run(begin, core), lambda: run(go_on, core), finish_all
+
+    def whole(act_on, cc):
+        act_on(None)
+
+    def q_other(plane, width):
+        return qfull.at[pl.ds(pl.multiple_of((plane * 2 + 1 - core) * band, band), band), :]
+
+    def g_part(cc):
+        return lambda plane, width: gcirc.at[
+            pl.ds(pl.multiple_of(cc * half + plane * band, band), band), pl.ds(0, width)
+        ]
 
     _, q_go_on, q_finish = gather(
-        q_part, q_send, q_recv,
-        lambda plane: qfull.at[
-            pl.ds(pl.multiple_of((plane * 2 + 1 - core) * band, band), band), :
-        ],
+        lambda plane, width: q_part(plane), q_send, q_recv, q_other, whole
     )
-    d_begin, d_go_on, d_finish = gather(lambda plane: plane_diags.at[plane], d_send, d_recv, None)
-    g_begin, g_go_on, g_finish = gather(
-        lambda plane: gcirc.at[pl.ds(pl.multiple_of(core * half + plane * band, band), band), :],
-        g_send, g_recv,
-        lambda plane: gcirc.at[
-            pl.ds(pl.multiple_of((1 - core) * half + plane * band, band), band), :
-        ],
+    d_begin, d_go_on, d_finish = gather(
+        lambda plane, width: plane_diags.at[plane], d_send, d_recv, None, whole
     )
+    g_begin, g_go_on, g_finish = gather(g_part(core), g_send, g_recv, g_part(1 - core), sized)
 
     def chips_of(k, sign):
         chips = []
@@ -372,29 +388,43 @@
         )
         store(n, direct, value)
 
-    def near_send(count, a):
+    def near_send(count, a, width):
         index = NEAR.index(count) * 3 + a + 1
+        cols = pl.ds(0, width)
         return remote(
-            gsend.at[along(count - FAR * a)], near_in.at[index], rs_send.at[index],
-            rs_recv.at[index], off(count),
+            gsend.at[along(count - FAR * a), :, cols], near_in.at[index, :, cols],
+            rs_send.at[index], rs_recv.at[index], off(count),
         )
 
     extra = 3 * len(NEAR)
-    last_send = remote(
-        gsend.at[along(8)], near_in.at[extra], rs_send.at[extra], rs_recv.at[extra], off(-3 * way)
-    )
-
-    def far_send(a):
+
+    def last_send(width):
+        cols = pl.ds(0, width)
+        return remote(
+            gsend.at[along(8), :, cols], near_in.at[extra, :, cols], rs_send.at[extra],
+            rs_recv.at[extra], off(-3 * way),
+        )
+
+    def far_send(a, width):
         index = extra + 1 + (a + 1) // 2
+        cols = pl.ds(0, width)
         return remote(
-            far_out.at[(a + 1) // 2], far_in.at[(a + 1) // 2], rs_send.at[index],
-            rs_recv.at[index], off(-FAR * a),
-        )
-
-    for count in NEAR:
-        for a in (1, -1):
-            near_send(count, a).start()
-    last_send.start()
+            far_out.at[(a + 1) // 2, :, cols], far_in.at[(a + 1) // 2, :, cols],
+            rs_send.at[index], rs_recv.at[index], off(-FAR * a),
+        )
+
+    def near_start(width):
+        for count in NEAR:
+            for a in (1, -1):
+                near_send(count, a, width).start()
+        last_send(width).start()
+
+    sized(near_start, core)
+
+    @pl.when(core == 1)
+    def _():
+        near_in[:, :, pl.ds(kept - 128, 128)] = jnp.zeros((extra + 1, band, 128), BF16)
+        far_in[:, :, pl.ds(kept - 128, 128)] = jnp.zeros((2, band, 128), BF16)
 
     squares = tall[...].astype(F32)
     squares = jnp.sum(squares * squares, axis=0, keepdims=True)
@@ -405,25 +435,44 @@
     def window(a):
         value = gpart[along(-FAR * a)]
         for count in NEAR:
-            near_send(count, a).wait_recv()
             value = value + near_in[NEAR.index(count) * 3 + a + 1].astype(F32)
         return value
 
-    upward, downward = window(1), window(-1)
-    last_send.wait_recv()
+    def near_wait(a):
+        def wait(width):
+            for count in NEAR:
+                near_send(count, a, width).wait_recv()
+            if a == -1:
+                last_send(width).wait_recv()
+
+        return wait
+
+    sized(near_wait(1), core)
+    upward = window(1)
+    sized(near_wait(-1), core)
+    downward = window(-1)
     more = near_in[extra].astype(F32)
     far_out[1] = (upward + jnp.where(core == 0, more, 0.0)).astype(BF16)
-    far_send(1).start()
     far_out[0] = (downward + jnp.where(core == 0, 0.0, more)).astype(BF16)
-    far_send(-1).start()
-    for count in NEAR:
-        near_send(count, 0).start()
+
+    def far_start(width):
+        for a in (1, -1):
+            far_send(a, width).start()
+        for count in NEAR:
+            near_send(count, 0, width).start()
+
+    sized(far_start, core)
     d_go_on()
+    sized(near_wait(0), core)
     value = window(0)
 
-    for a in (1, -1):
-        far_send(a).wait_recv()
-        value = value + far_in[(a + 1) // 2].astype(F32)
+
+    def far_wait(width):
+        for a in (1, -1):
+            far_send(a, width).wait_recv()
+
+    sized(far_wait, core)
+    value = value + far_in[1].astype(F32) + far_in[0].astype(F32)
     gcirc[pl.ds(pl.multiple_of(core * half + z * band, band), band), :] = value.astype(BF16)
     g_begin()
 
@@ -460,21 +509,27 @@
 
     lax.fori_loop(1, slots, settle, 0)
     pl.when(y_lo != core)(lambda: q_first(0).wait_send())
-    for count in NEAR:
-        for a in (1, -1, 0):
-            near_send(count, a).wait_send()
-    last_send.wait_send()
-    for a in (1, -1):
-        far_send(a).wait_send()
+
+    def sums_sent(width):
+        for count in NEAR:
+            for a in (1, -1, 0):
+                near_send(count, a, width).wait_send()
+        last_send(width).wait_send()
+        for a in (1, -1):
+            far_send(a, width).wait_send()
+
+    sized(sums_sent, core)
     q_finish()
     g_finish()
 
     for n in range(blocks):
         for k in range(kept // 128):
+            other = (n + k) % blocks
+            if 2 * k == blocks and n >= other:
+                continue
             piece = gcirc[n * 128 : (n + 1) * 128, k * 128 : (k + 1) * 128]
-            other = (n + k) % blocks
             gfull[n * 128 : (n + 1) * 128, other * 128 : (other + 1) * 128] = piece
-            if 0 < k < blocks - k:
+            if k > 0:
                 gfull[other * 128 : (other + 1) * 128, n * 128 : (n + 1) * 128] = piece.T
 
     damping = 0.1 * (jnp.sum(slot_traces[...], axis=0)[0:1, 0:1] / slots)

time: 85.3 us -> 82.4 us (0.966)
  Pallas kernels: 83.7 us -> 80.8 us
    pallas_call x1, Pallas kernels: 83.7 us -> 80.8 us  [per_device(): pl.pallas_call(functools.partial(kernel, planes), out_shape=jax.ShapeDtyp...]
where the time goes in v4:
time: 82.4 us; the launch traced here: 82.2 us
  Pallas kernels  80.8 us (98%)
  local copies, waits for them, and re-layouts  1.38 us (2%)
    pallas_call x1, Pallas kernels, per_device(): pl.pallas_call(functools.partial(kernel, planes), out_shape=jax.ShapeDtyp...  80.8 us

profile of v4, /device:TPU:1, one launch (start us, length us, event | category | flops | bytes accessed | tf_op | source)
XLA Modules:
  0.0 82.2 jit_solution(7782745214533316065)
XLA Ops:
  0.0 80.8 %shard_map.55 = f32[32,256]{1,0:T(8,128)} custom-call(s32[16]{0:T(128)} %slot_ref.1, s32[16]{0:T(128)} %len_ref.1, bf16[16,16,32,128]{3,2,1,0:T(8,128)(2,1)} %act_hbm.1, bf16[16,16,32,128]{3,2,1,0:T(8,128)(2,1)} %grad_hbm.1, f32[32,512]{1,0:T(8,128)} %bitcast.3), custom_call_target="tpu_custom_call" | custom-call | tf_op jit(solution)/shard_map/pallas_call | solution.py:636
  80.8 1.4 %copy.7 = f32[256,32]{0,1:T(8,128)} copy(f32[256,32]{0,1:T(8,128)} %bitcast.2) | data formatting | bytes 65536
